TPU v7x, 32 devices: a whole 2x2x4 slice. The times are simulated.
32 devices in a mesh: tm: 16 (over z, y, core), col: 2 (over x).
Axes of the slice: x: 2, y: 2, z: 4, core: 2. Of those that a mesh axis runs over, the one named last changes fastest.
Arguments:
- design: bfloat16 [2048, 2, 512], P('tm', None, 'col'), may hold values from -512 to 512
- filter_taps: bfloat16 [16, 2, 512], replicated, may hold values from -3 to 3
- segment: int32 [2048], P('tm'), may hold values from 0 to 15, never falling along the last dimension, each value on 1 to 256 neighbouring positions
- valid_flags: int32 [2048], P('tm'), may hold values 0 or 1
- weights: float32 [2, 2048], P(None, 'tm'), may hold values from 0.05 to 20
- block_ids: int32 [2], replicated, may hold values from 0 to 1, each once
Outputs:
- normals: float32 [512, 512], P('tm', 'col')
All inputs are finite; a program needn't handle non-finite values. No bound on the sum of `valid_flags` on one device may be relied on, other than what follows from the above.
Results may differ from a plain program's by a relative error of at most 0.0013.
Values may be sent and summed in bfloat16 or wider, within the bound.
No kernel may reach another device: no remote copies, remote signals or barrier semaphores. Data moves between devices by JAX's collectives and lax.ppermute only.
A program may use at most 64 MiB of HBM per device.

v0:
```python
import functools

import jax
import jax.numpy as jnp
from jax import lax
from jax.experimental import pallas as pl
from jax.experimental.pallas import tpu as pltpu
from jax.sharding import PartitionSpec as P

VMEM = pl.BlockSpec(memory_space=pltpu.VMEM)
SMEM = pl.BlockSpec(memory_space=pltpu.SMEM)
FIRST = (((0,), (0,)), ((), ()))
LIMIT = pltpu.CompilerParams(vmem_limit_bytes=24 * 2**20)
LONG = pl.CostEstimate(flops=2 * 10**10, bytes_accessed=2**20, transcendentals=0)


def rows_kernel(weights_ref, flags_ref, segment_ref, ids_ref, rows_ref, ids_out_ref):
    ids_out_ref[...] = ids_ref[...]
    rows_ref[0:2, :] = weights_ref[...] * flags_ref[...].astype(jnp.float32)
    rows_ref[2:3, :] = segment_ref[...].astype(jnp.float32)
    rows_ref[3:, :] = jnp.zeros_like(rows_ref[3:, :])


def prepare_kernel(taps_ref, design_ref, spread_ref, own_ref):
    own_ref[...] = design_ref[...]
    seg_count, _, tap_count = taps_ref.shape
    width = spread_ref.shape[1]
    row_count = design_ref.shape[0]
    tile = 128
    lane = lax.broadcasted_iota(jnp.int32, (tile, 2 * tile), 1)
    row = lax.broadcasted_iota(jnp.int32, (tile, 2 * tile), 0)
    taps = taps_ref[...].reshape(2 * seg_count, tap_count)
    component = lax.rem(lax.broadcasted_iota(jnp.int32, (2 * seg_count, 2 * tile), 0), 2)
    flips = [(lane == 2 * (tile - 1 - row) + k).astype(jnp.float32).astype(jnp.bfloat16) for k in range(2)]
    pieces = []
    for place in range(tap_count - tile, -1, -tile):
        part = taps[:, place : place + tile]
        first, second = (jnp.dot(part, flip, preferred_element_type=jnp.float32) for flip in flips)
        pieces.append(jnp.where(component == 0, first, second))
    pieces.append(jnp.zeros((2 * seg_count, width - 2 * tap_count), jnp.float32))
    spread = pltpu.roll(jnp.concatenate(pieces, axis=1), width - 2 * row_count - 2 * (tap_count - 1), 1)
    spread_ref[...] = spread.astype(jnp.bfloat16)


def choose_kernel(across_ref, own_ref, beside_ref, out_ref):
    out_ref[1] = beside_ref[...]
    index = lax.axis_index("tm")
    both = jnp.bitwise_and(jnp.bitwise_xor(index, lax.div(index, 2)), 1)

    @pl.when(both == 0)
    def _():
        out_ref[0] = across_ref[...]

    @pl.when(both == 1)
    def _():
        out_ref[0] = own_ref[...]


def toeplitz_kernel(rows_ref, rows_across_ref, spread_ref, out_ref, rows_here_ref):
    sources, width = spread_ref.shape
    depth, _, step = out_ref.shape
    row_count = step // 2
    later, epoch_block = epoch_block_here()
    rows = jnp.where(later, rows_across_ref[...], rows_ref[...])
    rows_here_ref[...] = rows
    segment = 2 * rows[2:3, :].astype(jnp.int32)
    source = lax.broadcasted_iota(jnp.int32, (sources, row_count), 0)
    column = lax.broadcasted_iota(jnp.int32, (row_count, width), 1)
    first_column = 2 * ((depth - 1) - epoch_block) * row_count
    for k in range(2):
        selector = (source == segment + k).astype(jnp.float32).astype(jnp.bfloat16)
        shifted = lax.dot_general(selector, spread_ref[...], FIRST, preferred_element_type=jnp.float32)
        shifted = pltpu.roll(shifted, 0, 1, stride=2, stride_axis=0)
        shifted = jnp.where(column >= first_column, shifted, 0.0).astype(jnp.bfloat16)
        for d in range(depth):
            place = (depth - 1 - d) * step
            out_ref[d, k * row_count : (k + 1) * row_count, :] = shifted[:, place : place + step]


def epoch_block_here():
    index, devices = lax.axis_index("tm"), lax.axis_size("tm")
    later = lax.rem(lax.div(index, 2), 2) == 0
    return later, jnp.where(later, lax.rem(index + 4, devices), index)


def sum_products(toeplitz_ref, pairs, total=None):
    for d, block_ref in pairs:
        row_count, _, width = block_ref.shape
        block = block_ref[...].reshape(2 * row_count, width)
        product = jnp.dot(toeplitz_ref[d], block, preferred_element_type=jnp.float32)
        total = product if total is None else total + product
    return total


def partial_kernel(toeplitz_ref, beside_ref, own_ref, across_ref, out_ref):
    later, _ = epoch_block_here()
    back = jnp.where(later, 4, 0)
    out_ref[...] = sum_products(toeplitz_ref, ((2, beside_ref), (back, own_ref), (4 - back, across_ref)))


def filtered_block(partial_ref, toeplitz_ref, swapped_ref):
    odd = lax.rem(lax.axis_index("tm"), 2)
    pairs = ((1 + 2 * odd, swapped_ref.at[1]), (3 - 2 * odd, swapped_ref.at[0]))
    return sum_products(toeplitz_ref, pairs, partial_ref[...]).astype(jnp.bfloat16).T


def filter_kernel(partial_ref, toeplitz_ref, swapped_ref, out_ref):
    block = filtered_block(partial_ref, toeplitz_ref, swapped_ref)
    out_ref[...] = block.reshape(out_ref.shape)


def filter_split_kernel(partial_ref, toeplitz_ref, swapped_ref, all_ref, here_ref, there_ref):
    block = filtered_block(partial_ref, toeplitz_ref, swapped_ref)
    width, length = block.shape
    all_ref[...] = block
    groups, _, rows_out, _ = here_ref.shape
    block = block.reshape(groups, 2, 2, rows_out, length)
    place = lax.rem(lax.div(lax.axis_index("tm"), 2), 2)
    for side in range(2):

        @pl.when(place == side)
        def _(side=side):
            here_ref[...] = block[:, side]
            there_ref[...] = block[:, 1 - side]


def split_scale_kernel(back, *refs):
    *held_refs, rows_ref, rows_beside_ref, other_ref, scaled_ref = refs
    held_refs = [held_refs[i] for i in back]
    for unit, (ref, lines_ref) in enumerate(zip(held_refs[:2], (rows_ref, rows_beside_ref))):
        weight = jnp.concatenate([lines_ref[0:1], lines_ref[1:2]], axis=1)
        scaled_ref[unit] = (ref[...].astype(jnp.float32) * weight).astype(jnp.bfloat16)
    split_gram(held_refs, scaled_ref, other_ref, 1)


def split_gram_kernel(back, scaled_ref, *refs):
    *held_refs, mine_ref = refs
    held_refs = [held_refs[i] for i in back]
    split_gram(held_refs, scaled_ref, mine_ref, 0)


def split_gram(held_refs, scaled_ref, out_ref, flip):
    index, column = lax.axis_index("tm"), lax.axis_index("col")
    place = lax.rem(lax.div(index, 2), 2)
    parity = jnp.bitwise_xor(lax.rem(index, 2), flip)
    all_refs, half_refs = held_refs[:2], held_refs[2:]
    groups, _, rows_out, length = half_refs[0].shape
    first = place * 2 * rows_out + parity * rows_out
    for block in range(2):
        total = None
        for unit in range(2):
            if block == 0:
                pieces = [
                    all_refs[unit][pl.ds(pl.multiple_of(g * 4 * rows_out + first, rows_out), rows_out), :]
                    for g in range(groups)
                ]
                rows = jnp.concatenate(pieces, axis=0)
            else:
                rows = half_refs[unit][:, parity].reshape(groups * rows_out, length)
            product = lax.dot_general(
                rows, scaled_ref[unit], (((1,), (1,)), ((), ())), preferred_element_type=jnp.float32
            )
            total = product if total is None else total + product
        at = jnp.bitwise_xor(column, block) * groups
        out_ref[pl.ds(at, groups)] = total.reshape(groups, rows_out, total.shape[1])


def early_kernel(every_ref, rows_ref, scaled_ref, other_ref, mine_ref):
    scaled_ref[...] = scaled_block(every_ref, rows_ref)
    for out_ref, flip in ((other_ref, 1), (mine_ref, 0)):
        out_ref[...] = product_of(whole_rows(every_ref, out_ref.shape[:2], flip), scaled_ref).reshape(out_ref.shape)


def late_kernel(
    beside_ref, both_ref, column_ref, rows_beside_ref, scaled_ref, early_ref, out_ref, scaled_beside_ref
):
    scaled_beside_ref[...] = scaled_block(beside_ref, rows_beside_ref)
    late_sums(1, beside_ref, both_ref, column_ref, scaled_ref, early_ref, scaled_beside_ref, out_ref)


def late_mine_kernel(*refs):
    late_sums(0, *refs)


def late_sums(flip, beside_ref, both_ref, column_ref, scaled_ref, early_ref, scaled_beside_ref, out_ref):
    groups, rows_out, width = early_ref.shape
    column = lax.axis_index("col")
    parity = jnp.bitwise_xor(lax.rem(lax.axis_index("tm"), 2), flip)
    same = product_of(whole_rows(beside_ref, (groups, rows_out), flip), scaled_beside_ref)
    out_ref[pl.ds(column * groups, groups)] = early_ref[...] + same.reshape(early_ref.shape)
    halves = [ref[:, parity].reshape(groups * rows_out, width) for ref in (column_ref, both_ref)]
    cross = product_of(halves[0], scaled_ref) + product_of(halves[1], scaled_beside_ref)
    out_ref[pl.ds((1 - column) * groups, groups)] = cross.reshape(early_ref.shape)


def scaled_block(block_ref, rows_ref):
    weight = jnp.concatenate([rows_ref[0:1], rows_ref[1:2]], axis=1)
    return (block_ref[...].astype(jnp.float32) * weight).astype(jnp.bfloat16)


def whole_rows(ref, shape, flip):
    groups, rows_out = shape
    index = lax.axis_index("tm")
    parity = jnp.bitwise_xor(lax.rem(index, 2), flip)
    first = (lax.rem(lax.div(index, 2), 2) * 2 + parity) * rows_out
    pieces = [
        ref[pl.ds(pl.multiple_of(g * 4 * rows_out + first, rows_out), rows_out), :] for g in range(groups)
    ]
    return jnp.concatenate(pieces, axis=0)


def product_of(rows, scaled_ref):
    return lax.dot_general(
        rows, scaled_ref[...], (((1,), (1,)), ((), ())), preferred_element_type=jnp.float32
    )


def scale_kernel(ids_ref, rows_ref, rows_beside_ref, *refs):
    *held_refs, other_ref, scaled_ref = refs
    columns = len(held_refs) // 2
    width, length = scaled_ref.shape[1:]
    column = lax.axis_index("col")
    for unit, ref in enumerate((rows_ref, rows_beside_ref)):
        weight = jnp.concatenate([ref[0:1], ref[1:2]], axis=1)
        for d in range(columns):

            @pl.when(ids_ref[lax.rem(column + d, columns)] == column)
            def _(d=d, unit=unit, weight=weight):
                values = held_refs[2 * d + unit][...].reshape(width, length).astype(jnp.float32)
                scaled_ref[unit] = (values * weight).astype(jnp.bfloat16)

    gram(ids_ref, held_refs, scaled_ref, other_ref, 1)


def gram_kernel(ids_ref, scaled_ref, *refs):
    *held_refs, mine_ref = refs
    gram(ids_ref, held_refs, scaled_ref, mine_ref, 0)


def gram(ids_ref, held_refs, scaled_ref, out_ref, flip):
    columns = len(held_refs) // 2
    index, column = lax.axis_index("tm"), lax.axis_index("col")
    beside = lax.rem(lax.div(index, 2), 2)
    parity = jnp.bitwise_xor(lax.rem(index, 2), flip)
    length = scaled_ref.shape[2]
    groups, _, _, rows_out, _ = held_refs[0].shape
    for d in range(columns):
        total = None
        for unit in range(2):
            rows = held_refs[2 * d + unit][:, beside, parity].reshape(groups * rows_out, length)
            product = lax.dot_general(
                rows, scaled_ref[unit], (((1,), (1,)), ((), ())), preferred_element_type=jnp.float32
            )
            total = product if total is None else total + product
        place = pl.ds(ids_ref[lax.rem(column + d, columns)] * groups, groups)
        out_ref[place] = total.reshape(groups, rows_out, total.shape[1])


def body(design, filter_taps, segment, valid_flags, weights, block_ids):
    row_count = design.shape[0]
    block_width = design.shape[2]
    tap_count = filter_taps.shape[2]
    seg_count = filter_taps.shape[0]
    devices = lax.axis_size("tm")
    columns = lax.axis_size("col")
    rows_out = columns * block_width // devices
    halo_depth = (tap_count - 2) // row_count + 1
    if halo_depth != 4 or devices % 4:
        raise ValueError("halo depth")
    index = lax.axis_index("tm")
    swap = [(i, i ^ 1) for i in range(devices)]
    beside_pairs = [(i, i ^ 2) for i in range(devices)]
    across_pairs = [(i, (i + (4 if i & 2 else -4)) % devices) for i in range(devices)]

    across = lax.ppermute(design, "tm", across_pairs)
    rows, ids = pl.pallas_call(
        rows_kernel,
        out_shape=[
            jax.ShapeDtypeStruct((8, row_count), jnp.float32),
            jax.ShapeDtypeStruct((1, columns), jnp.int32),
        ],
        in_specs=[VMEM] * 4,
        out_specs=[VMEM] * 2,
        compiler_params=LIMIT,
        name="rows",
    )(weights, valid_flags.reshape(1, row_count), segment.reshape(1, row_count), block_ids.reshape(1, columns))
    rows_pairs = [(i, i ^ 4 if i & 2 else (i - 4) % devices) for i in range(devices)]
    rows_across = lax.ppermute(rows, "tm", rows_pairs)
    beside = lax.ppermute(design, "tm", beside_pairs)
    spread, own = pl.pallas_call(
        prepare_kernel,
        out_shape=[
            jax.ShapeDtypeStruct((2 * seg_count, 2 * (halo_depth + 1) * row_count), jnp.bfloat16),
            jax.ShapeDtypeStruct(design.shape, design.dtype),
        ],
        in_specs=[VMEM] * 2,
        out_specs=[VMEM] * 2,
        compiler_params=LIMIT,
        name="prepare",
    )(filter_taps, design)
    toeplitz, rows_here = pl.pallas_call(
        toeplitz_kernel,
        out_shape=[
            jax.ShapeDtypeStruct((halo_depth + 1, 2 * row_count, 2 * row_count), jnp.bfloat16),
            jax.ShapeDtypeStruct(rows.shape, rows.dtype),
        ],
        in_specs=[VMEM] * 3,
        out_specs=[VMEM] * 2,
        compiler_params=LIMIT,
        cost_estimate=LONG,
        name="toeplitz",
    )(rows, rows_across, spread)
    chosen = pl.pallas_call(
        choose_kernel,
        out_shape=jax.ShapeDtypeStruct((2, *design.shape), design.dtype),
        in_specs=[VMEM] * 3,
        out_specs=VMEM,
        compiler_params=LIMIT,
        name="choose",
    )(across, own, beside)
    swapped = lax.ppermute(chosen, "tm", swap)
    partial = pl.pallas_call(
        partial_kernel,
        out_shape=jax.ShapeDtypeStruct((2 * row_count, block_width), jnp.float32),
        in_specs=[VMEM] * 4,
        out_specs=VMEM,
        compiler_params=LIMIT,
        name="partial",
    )(toeplitz, beside, own, across)
    split = columns == 2 and rows_out % 16 == 0 and block_width % (4 * rows_out) == 0
    finish = finish_two if split else finish_any
    total = finish(rows_here, (partial, toeplitz, swapped), ids.reshape(columns), rows_out, swap, beside_pairs)
    return total * (1.0 / (2.0 * row_count * devices))


def core_sum(mine, other, swap):
    return mine + lax.ppermute(other, "tm", swap)


def sum_over_groups(total, stride, turns=(3, 1, 2)):
    devices = lax.axis_size("tm")
    index = lax.axis_index("tm")
    left = total.shape[0]
    while left > 1:
        group = 4 if left % 4 == 0 else 2
        shares = total.reshape(left // group, group, *total.shape[1:])
        place = index // stride % group

        def share(j):
            return lax.dynamic_index_in_dim(shares, j, 1, keepdims=False)

        total = share(place)
        for d in turns if group == 4 else (1,):
            total = total + lax.ppermute(share(place ^ d), "tm", [(i, i ^ (d * stride)) for i in range(devices)])
        stride, left = stride * group, left // group
    return total[0]


def finish_two(rows_here, blocks, block_ids, rows_out, swap, beside_pairs):
    devices = lax.axis_size("tm")
    length, width = blocks[0].shape
    groups = width // rows_out // 4
    half = jax.ShapeDtypeStruct((groups, 2, rows_out, length), jnp.bfloat16)
    every, here, there = pl.pallas_call(
        filter_split_kernel,
        out_shape=[jax.ShapeDtypeStruct((width, length), jnp.bfloat16), half, half],
        in_specs=[VMEM] * 3,
        out_specs=[VMEM] * 3,
        compiler_params=LIMIT,
        name="filter",
    )(*blocks)

    def sums(own_block):
        def run(every, here, there, rows_here):
            across_column = [(0, 1), (1, 0)]
            both = [(i * 2 + c, (i ^ 2) * 2 + 1 - c) for i in range(devices) for c in range(2)]
            if own_block:
                held = (
                    every,
                    lax.ppermute(every, "tm", beside_pairs),
                    lax.ppermute(here, "col", across_column),
                    lax.ppermute(there, ("tm", "col"), both),
                )
            else:
                held = (
                    lax.ppermute(every, "col", across_column),
                    lax.ppermute(every, ("tm", "col"), both),
                    here,
                    lax.ppermute(there, "tm", beside_pairs),
                )
            order = (1, 3, 2, 0) if own_block else (3, 0, 1, 2)
            back = tuple(order.index(i) for i in range(4))
            share = jax.ShapeDtypeStruct((2 * groups, rows_out, width), jnp.float32)
            other, scaled = pl.pallas_call(
                functools.partial(split_scale_kernel, back),
                out_shape=[share, jax.ShapeDtypeStruct((2, width, length), jnp.bfloat16)],
                in_specs=[VMEM] * 6,
                out_specs=[VMEM] * 2,
                compiler_params=LIMIT,
                name="scale",
            )(*(held[i] for i in order), rows_here, lax.ppermute(rows_here, "tm", beside_pairs))
            mine = pl.pallas_call(
                functools.partial(split_gram_kernel, back),
                out_shape=share,
                in_specs=[VMEM] * 5,
                out_specs=VMEM,
                compiler_params=LIMIT,
                name="gram",
            )(scaled, *(held[i] for i in order))
            return sum_over_groups(core_sum(mine, other, swap), 4, (2, 1, 3) if own_block else (3, 1, 2))

        return run

    def sums_own(every, here, there, rows_here):
        beside_every = lax.ppermute(every, "tm", beside_pairs)
        column_half = lax.ppermute(here, "col", [(0, 1), (1, 0)])
        both = [(i * 2 + c, (i ^ 2) * 2 + 1 - c) for i in range(devices) for c in range(2)]
        both_half = lax.ppermute(there, ("tm", "col"), both)
        rows_beside = lax.ppermute(rows_here, "tm", beside_pairs)
        share = jax.ShapeDtypeStruct((groups, rows_out, width), jnp.float32)
        shares = jax.ShapeDtypeStruct((2 * groups, rows_out, width), jnp.float32)
        block = jax.ShapeDtypeStruct((width, length), jnp.bfloat16)
        scaled, other_early, mine_early = pl.pallas_call(
            early_kernel,
            out_shape=[block, share, share],
            in_specs=[VMEM] * 2,
            out_specs=[VMEM] * 3,
            compiler_params=LIMIT,
            name="early",
        )(every, rows_here)
        other, scaled_beside = pl.pallas_call(
            late_kernel,
            out_shape=[shares, block],
            in_specs=[VMEM] * 6,
            out_specs=[VMEM] * 2,
            compiler_params=LIMIT,
            name="late",
        )(beside_every, both_half, column_half, rows_beside, scaled, other_early)
        mine = pl.pallas_call(
            late_mine_kernel,
            out_shape=shares,
            in_specs=[VMEM] * 6,
            out_specs=VMEM,
            compiler_params=LIMIT,
            name="late_mine",
        )(beside_every, both_half, column_half, scaled, mine_early, scaled_beside)
        return sum_over_groups(core_sum(mine, other, swap), 4, (2, 1, 3))

    return lax.cond(block_ids[0] == 0, sums_own, sums(False), every, here, there, rows_here)


def finish_any(rows_here, blocks, block_ids, rows_out, swap, beside_pairs):
    devices, columns = lax.axis_size("tm"), lax.axis_size("col")
    length, width = blocks[0].shape
    filtered = pl.pallas_call(
        filter_kernel,
        out_shape=jax.ShapeDtypeStruct((width // rows_out // 4, 2, 2, rows_out, length), jnp.bfloat16),
        in_specs=[VMEM] * 3,
        out_specs=VMEM,
        compiler_params=LIMIT,
        name="filter",
    )(*blocks)
    held = []
    for d in range(columns):
        for e in range(2):
            pairs = [
                (i * columns + (c + d) % columns, (i ^ 2 * e) * columns + c)
                for i in range(devices)
                for c in range(columns)
            ]
            held.append(lax.ppermute(filtered, ("tm", "col"), pairs) if d or e else filtered)
    rows_beside = lax.ppermute(rows_here, "tm", beside_pairs)
    share = jax.ShapeDtypeStruct((devices // 4, rows_out, width), jnp.float32)
    other, scaled = pl.pallas_call(
        scale_kernel,
        out_shape=[share, jax.ShapeDtypeStruct((2, width, length), jnp.bfloat16)],
        in_specs=[SMEM] + [VMEM] * (2 + 2 * columns),
        out_specs=[VMEM] * 2,
        compiler_params=LIMIT,
        name="scale",
    )(block_ids, rows_here, rows_beside, *held)
    mine = pl.pallas_call(
        gram_kernel,
        out_shape=share,
        in_specs=[SMEM] + [VMEM] * (1 + 2 * columns),
        out_specs=VMEM,
        compiler_params=LIMIT,
        name="gram",
    )(block_ids, scaled, *held)
    return sum_over_groups(core_sum(mine, other, swap), 4)


def solution(mesh):
    return jax.shard_map(
        body,
        mesh=mesh,
        in_specs=(P("tm", None, "col"), P(), P("tm"), P("tm"), P(None, "tm"), P()),
        out_specs=P("tm", "col"),
        check_vma=False,
    )
```

profile of v0, /device:TPU:0, one launch (start us, length us, event | category | flops | bytes accessed | tf_op | source)
XLA Modules:
  0.0 29.9 jit_solution(15131501751462993636)
XLA Ops:
  0.0 5.0 %collective-permute-start.18 = (bf16[128,2,256]{2,1,0:T(2,128)(2,1)}, bf16[128,2,256]{2,1,0:T(2,128)(2,1)S(1)}, u32[]{:S(2)}, u32[]{:S(2)}) collective-permute-start(bf16[128,2,256]{2,1,0:T(2,128)(2,1)} %design_ref.1), channel_id=1, source_target_pairs={{0,24},{2,26},{4,12},{6,14},{8,0},{10,2},{12,20},{14,22},{16,8},{1... | collective-permute-start | bytes 393224 | tf_op jit(solution)/shard_map/ppermute | solution.py:275
  5.1 0.6 %copy-done.4 = s32[128]{0:T(128)S(1)} copy-done((s32[128]{0:T(128)S(1)}, s32[128]{0:T(128)}, u32[]{:S(2)}) %copy-start.4) | copy-done | bytes 536
  5.7 0.0 copy-done.5
  5.7 0.0 copy-done.2
  5.8 1.8 %collective-permute-start.16 = (f32[8,128]{1,0:T(8,128)S(1)}, f32[8,128]{1,0:T(8,128)S(1)}, u32[]{:S(2)}, u32[]{:S(2)}) collective-permute-start(f32[8,128]{1,0:T(8,128)S(1)} %get-tuple-element.49.rows_ref), channel_id=1, source_target_pairs={{0,24},{2,26},{4,12},{6,14},{8,0},{10,2},{12,4},{14,6},{16,8},{18,... | collective-permute-start | bytes 12296 | tf_op jit(solution)/shard_map/ppermute | solution.py:288
  7.6 0.9 %copy-done = bf16[128,2,256]{2,1,0:T(2,128)(2,1)S(1)} copy-done((bf16[128,2,256]{2,1,0:T(2,128)(2,1)S(1)}, bf16[128,2,256]{2,1,0:T(2,128)(2,1)}, u32[]{:S(2)}) %copy-start) | copy-done | bytes 131096
  8.5 0.8 %copy-done.1 = bf16[16,2,512]{2,1,0:T(2,128)(2,1)S(1)} copy-done((bf16[16,2,512]{2,1,0:T(2,128)(2,1)S(1)}, bf16[16,2,512]{2,1,0:T(2,128)(2,1)}, u32[]{:S(2)}) %copy-start.1) | copy-done | bytes 32792
  9.3 0.3 prepare.1
  9.6 0.7 %collective-permute-done.17.beside_ref = bf16[128,2,256]{2,1,0:T(2,128)(2,1)S(1)} collective-permute-done((bf16[128,2,256]{2,1,0:T(2,128)(2,1)}, bf16[128,2,256]{2,1,0:T(2,128)(2,1)S(1)}, u32[]{:S(2)}, u32[]{:S(2)}) %collective-permute-start.17) | collective-permute-done | bytes 131104 | tf_op jit(solution)/shard_map/ppermute | solution.py:289
  10.3 0.1 collective-permute-start.19
  10.3 0.5 %toeplitz.1 = (bf16[5,256,256]{2,1,0:T(8,128)(2,1)S(1)}, f32[8,128]{1,0:T(8,128)S(1)}) custom-call(f32[8,128]{1,0:T(8,128)S(1)} %get-tuple-element.49.rows_ref, f32[8,128]{1,0:T(8,128)S(1)} %collective-permute-done.16.rows_across_ref, bf16[32,1280]{1,0:T(8,128)(2,1)S(1)} %get-tuple-element.50.spread_ref), custom_call_target="tpu_custom_call" | custom-call | flops 20000000000 | bytes 1048576 | tf_op jit(solution)/shard_map/toeplitz/pallas_call | solution.py:301
  10.8 0.3 %partial.1.partial_ref = f32[256,256]{1,0:T(8,128)S(1)} custom-call(bf16[5,256,256]{2,1,0:T(8,128)(2,1)S(1)} %get-tuple-element.51.toeplitz_ref, bf16[128,2,256]{2,1,0:T(2,128)(2,1)S(1)} %collective-permute-done.17.beside_ref, bf16[128,2,256]{2,1,0:T(2,128)(2,1)S(1)} %get-tuple-element.52.own_ref, bf16[128,2,256]{2,1,0:T(2,128)(2,1)S(1)} %collective-permute-done.18.across_ref), custom_call_target="tpu_custom_call" | custom-call | tf_op jit(solution)/shard_map/partial/pallas_call | solution.py:322
  11.2 0.7 %collective-permute-done.19.swapped_ref = bf16[2,128,2,256]{3,2,1,0:T(2,128)(2,1)S(1)} collective-permute-done((bf16[2,128,2,256]{3,2,1,0:T(2,128)(2,1)S(1)}, bf16[2,128,2,256]{3,2,1,0:T(2,128)(2,1)S(1)}, u32[]{:S(2)}, u32[]{:S(2)}) %collective-permute-start.19) | collective-permute-done | bytes 262176 | tf_op jit(solution)/shard_map/ppermute | solution.py:321
  11.9 0.3 %filter.1 = (bf16[256,256]{1,0:T(8,128)(2,1)S(1)}, bf16[2,2,32,256]{3,2,1,0:T(8,128)(2,1)S(1)}, bf16[2,2,32,256]{3,2,1,0:T(8,128)(2,1)S(1)}) custom-call(f32[256,256]{1,0:T(8,128)S(1)} %partial.1.partial_ref, bf16[5,256,256]{2,1,0:T(8,128)(2,1)S(1)} %get-tuple-element.51.toeplitz_ref, bf16[2,128,2,256]{3,2,1,0:T(2,128)(2,1)S(1)} %collective-permute-done.19.swapped_ref), custom_call_target="tpu_custom_call" | custom-call | tf_op jit(solution)/shard_map/filter/pallas_call | solution.py:364
  12.2 17.1 %conditional.1 = (f32[32,256]{1,0:T(8,128)S(1)}) conditional(s32[]{:T(128)} %bitcast.5, (bf16[2,2,32,256]{3,2,1,0:T(8,128)(2,1)S(1)}, bf16[256,256]{1,0:T(8,128)(2,1)S(1)}, f32[8,128]{1,0:T(8,128)S(1)}, bf16[2,2,32,256]{3,2,1,0:T(8,128)(2,1)S(1)}) %tuple.11, (bf16[256,256]{1,0:T(8,128)(2,1)S(1)}, bf16[2,2,32,256]{3,2,1,0:T(8,128)(2,1)S(1)}, ...), branch_computations={%region_0.1_spmd, %region_1.2_spmd} | conditional | flops 57388 | bytes 2999079 | solution.py:449
  12.2 1.4 %collective-permute-start.2 = (bf16[256,256]{1,0:T(8,128)(2,1)S(1)}, bf16[256,256]{1,0:T(8,128)(2,1)S(1)}, u32[]{:S(2)}, u32[]{:S(2)}) collective-permute-start(bf16[256,256]{1,0:T(8,128)(2,1)S(1)} %get-tuple-element.25), channel_id=1, source_target_pairs={{0,5},{1,4},{2,7},{3,6},{4,1},{5,0},{6,3},{7,2},{8,13},{9,12},{10,... | collective-permute-start | bytes 393224 | tf_op jit(solution)/shard_map/cond/branch_0_fun/ppermute | solution.py:387
  13.6 0.5 %collective-permute-start.1 = (bf16[256,256]{1,0:T(8,128)(2,1)S(1)}, bf16[256,256]{1,0:T(8,128)(2,1)S(1)}, u32[]{:S(2)}, u32[]{:S(2)}) collective-permute-start(bf16[256,256]{1,0:T(8,128)(2,1)S(1)} %get-tuple-element.25), channel_id=1, source_target_pairs={{0,1},{1,0},{2,3},{3,2},{4,5},{5,4},{6,7},{7,6},{8,9},{9,8},{10,11... | collective-permute-start | bytes 393224 | tf_op jit(solution)/shard_map/cond/branch_0_fun/ppermute | solution.py:386
  14.2 1.6 %collective-permute-start = (bf16[2,2,32,256]{3,2,1,0:T(8,128)(2,1)S(1)}, bf16[2,2,32,256]{3,2,1,0:T(8,128)(2,1)S(1)}, u32[]{:S(2)}, u32[]{:S(2)}) collective-permute-start(bf16[2,2,32,256]{3,2,1,0:T(8,128)(2,1)S(1)} %get-tuple-element.24), channel_id=1, source_target_pairs={{0,4},{2,6},{4,0},{6,2},{8,12},{10,14},{12,8},{14,10},{16,20},{18,... | collective-permute-start | bytes 196616 | tf_op jit(solution)/shard_map/cond/branch_0_fun/ppermute | solution.py:389
  15.8 0.4 %collective-permute-start.3 = (f32[8,128]{1,0:T(8,128)S(1)}, f32[8,128]{1,0:T(8,128)S(1)}, u32[]{:S(2)}, u32[]{:S(2)}) collective-permute-start(f32[8,128]{1,0:T(8,128)S(1)} %get-tuple-element.27.refs_4_), channel_id=1, source_target_pairs={{0,4},{2,6},{4,0},{6,2},{8,12},{10,14},{12,8},{14,10},{16,20},{18,... | collective-permute-start | bytes 12296 | tf_op jit(solution)/shard_map/cond/branch_0_fun/ppermute | solution.py:401
  16.2 4.0 %collective-permute-done.3.refs_5_ = f32[8,128]{1,0:T(8,128)S(1)} collective-permute-done((f32[8,128]{1,0:T(8,128)S(1)}, f32[8,128]{1,0:T(8,128)S(1)}, u32[]{:S(2)}, u32[]{:S(2)}) %collective-permute-start.3) | collective-permute-done | bytes 4128 | tf_op jit(solution)/shard_map/cond/branch_0_fun/ppermute | solution.py:401
  20.2 0.2 collective-permute-done.1.refs_1_
  20.4 0.3 scale.1
  20.7 0.1 collective-permute-start.4
  20.8 0.3 gram.1
  21.1 1.0 %collective-permute-done.4 = f32[4,32,256]{2,1,0:T(8,128)S(1)} collective-permute-done((f32[4,32,256]{2,1,0:T(8,128)S(1)}, f32[4,32,256]{2,1,0:T(8,128)S(1)}, u32[]{:S(2)}, u32[]{:S(2)}) %collective-permute-start.4) | collective-permute-done | bytes 131104 | tf_op jit(solution)/shard_map/cond/branch_0_fun/ppermute | solution.py:337
  22.1 2.2 %collective-permute-start.5 = (f32[1,32,256]{2,1,0:T(8,128)S(1)}, f32[1,32,256]{2,1,0:T(8,128)S(1)}, u32[]{:S(2)}, u32[]{:S(2)}) collective-permute-start(f32[1,32,256]{2,1,0:T(8,128)S(1)} %get-tuple-element.57), channel_id=1, source_target_pairs={{0,24},{2,26},{4,28},{6,30},{8,16},{10,18},{12,20},{14,22},{16,8},... | collective-permute-start | bytes 98312 | tf_op jit(solution)/shard_map/cond/branch_0_fun/ppermute | solution.py:354
  24.3 0.7 %collective-permute-start.7 = (f32[1,32,256]{2,1,0:T(8,128)S(1)}, f32[1,32,256]{2,1,0:T(8,128)S(1)}, u32[]{:S(2)}, u32[]{:S(2)}) collective-permute-start(f32[1,32,256]{2,1,0:T(8,128)S(1)} %get-tuple-element.58), channel_id=1, source_target_pairs={{0,16},{2,18},{4,20},{6,22},{8,24},{10,26},{12,28},{14,30},{16,0},... | collective-permute-start | bytes 98312 | tf_op jit(solution)/shard_map/cond/branch_0_fun/ppermute | solution.py:354
  25.0 1.6 %collective-permute-start.6 = (f32[1,32,256]{2,1,0:T(8,128)S(1)}, f32[1,32,256]{2,1,0:T(8,128)S(1)}, u32[]{:S(2)}, u32[]{:S(2)}) collective-permute-start(f32[1,32,256]{2,1,0:T(8,128)S(1)} %get-tuple-element.59), channel_id=1, source_target_pairs={{0,8},{2,10},{4,12},{6,14},{8,0},{10,2},{12,4},{14,6},{16,24},{18,... | collective-permute-start | bytes 98312 | tf_op jit(solution)/shard_map/cond/branch_0_fun/ppermute | solution.py:354
  26.6 1.5 %collective-permute-done.5 = f32[1,32,256]{2,1,0:T(8,128)S(1)} collective-permute-done((f32[1,32,256]{2,1,0:T(8,128)S(1)}, f32[1,32,256]{2,1,0:T(8,128)S(1)}, u32[]{:S(2)}, u32[]{:S(2)}) %collective-permute-start.5) | collective-permute-done | bytes 32800 | tf_op jit(solution)/shard_map/cond/branch_0_fun/ppermute | solution.py:354
  28.0 1.2 %collective-permute-done.7 = f32[1,32,256]{2,1,0:T(8,128)S(1)} collective-permute-done((f32[1,32,256]{2,1,0:T(8,128)S(1)}, f32[1,32,256]{2,1,0:T(8,128)S(1)}, u32[]{:S(2)}, u32[]{:S(2)}) %collective-permute-start.7) | collective-permute-done | bytes 32800 | tf_op jit(solution)/shard_map/cond/branch_0_fun/ppermute | solution.py:354
  29.3 0.0 collective-permute-done.6
  29.3 0.6 %broadcast_multiply_fusion = f32[32,256]{1,0:T(8,128)} fusion(f32[32,256]{1,0:T(8,128)S(1)} %get-tuple-element.63), kind=kLoop, calls=%fused_computation.8 | loop fusion | flops 8192 | bytes 65536 | tf_op jit(solution)/shard_map/mul | solution.py:333
  (17 shorter events, 0.1 us)
Async XLA Ops:
  0.0 9.6 %collective-permute-start.18 = (bf16[128,2,256]{2,1,0:T(2,128)(2,1)}, bf16[128,2,256]{2,1,0:T(2,128)(2,1)S(1)}, u32[]{:S(2)}, u32[]{:S(2)}) collective-permute-start(bf16[128,2,256]{2,1,0:T(2,128)(2,1)} %design_ref.1), channel_id=1, source_target_pairs={{0,24},{2,26},{4,12},{6,14},{8,0},{10,2},{12,20},{14,22},{16,8},{1... | collective-permute-start | bytes 393224 | tf_op jit(solution)/shard_map/ppermute | solution.py:275
  5.0 5.2 %collective-permute-start.17 = (bf16[128,2,256]{2,1,0:T(2,128)(2,1)}, bf16[128,2,256]{2,1,0:T(2,128)(2,1)S(1)}, u32[]{:S(2)}, u32[]{:S(2)}) collective-permute-start(bf16[128,2,256]{2,1,0:T(2,128)(2,1)} %design_ref.1), channel_id=1, source_target_pairs={{0,4},{2,6},{4,0},{6,2},{8,12},{10,14},{12,8},{14,10},{16,20},{18,... | collective-permute-start | bytes 393224 | tf_op jit(solution)/shard_map/ppermute | solution.py:289
  5.1 0.7 %copy-start.4 = (s32[128]{0:T(128)S(1)}, s32[128]{0:T(128)}, u32[]{:S(2)}) copy-start(s32[128]{0:T(128)} %param.10) | copy-start | bytes 1540
  5.1 0.7 %copy-start.5 = (s32[2]{0:T(128)S(1)}, s32[2]{0:T(128)}, u32[]{:S(2)}) copy-start(s32[2]{0:T(128)} %param.13) | copy-start | bytes 28
  5.1 0.7 %copy-start.2 = (f32[2,128]{1,0:T(2,128)S(1)}, f32[2,128]{1,0:T(2,128)}, u32[]{:S(2)}) copy-start(f32[2,128]{1,0:T(2,128)} %weights_ref.1) | copy-start | bytes 3076
  5.1 0.7 %copy-start.3 = (s32[128]{0:T(128)S(1)}, s32[128]{0:T(128)}, u32[]{:S(2)}) copy-start(s32[128]{0:T(128)} %param.11) | copy-start | bytes 1540
  5.8 4.6 %collective-permute-start.16 = (f32[8,128]{1,0:T(8,128)S(1)}, f32[8,128]{1,0:T(8,128)S(1)}, u32[]{:S(2)}, u32[]{:S(2)}) collective-permute-start(f32[8,128]{1,0:T(8,128)S(1)} %get-tuple-element.49.rows_ref), channel_id=1, source_target_pairs={{0,24},{2,26},{4,12},{6,14},{8,0},{10,2},{12,4},{14,6},{16,8},{18,... | collective-permute-start | bytes 12296 | tf_op jit(solution)/shard_map/ppermute | solution.py:288
  7.6 0.9 %copy-start = (bf16[128,2,256]{2,1,0:T(2,128)(2,1)S(1)}, bf16[128,2,256]{2,1,0:T(2,128)(2,1)}, u32[]{:S(2)}) copy-start(bf16[128,2,256]{2,1,0:T(2,128)(2,1)} %design_ref.1) | copy-start | bytes 393220
  8.5 0.8 %copy-start.1 = (bf16[16,2,512]{2,1,0:T(2,128)(2,1)S(1)}, bf16[16,2,512]{2,1,0:T(2,128)(2,1)}, u32[]{:S(2)}) copy-start(bf16[16,2,512]{2,1,0:T(2,128)(2,1)} %taps_ref.1) | copy-start | bytes 98308
  10.3 1.6 %collective-permute-start.19 = (bf16[2,128,2,256]{3,2,1,0:T(2,128)(2,1)S(1)}, bf16[2,128,2,256]{3,2,1,0:T(2,128)(2,1)S(1)}, u32[]{:S(2)}, u32[]{:S(2)}) collective-permute-start(bf16[2,128,2,256]{3,2,1,0:T(2,128)(2,1)S(1)} %choose.1), channel_id=1, source_target_pairs={{0,2},{2,0},{4,6},{6,4},{8,10},{10,8},{12,14},{14,12},{16,18},{18,... | collective-permute-start | bytes 786440 | tf_op jit(solution)/shard_map/ppermute | solution.py:321
  12.2 8.0 %collective-permute-start.2 = (bf16[256,256]{1,0:T(8,128)(2,1)S(1)}, bf16[256,256]{1,0:T(8,128)(2,1)S(1)}, u32[]{:S(2)}, u32[]{:S(2)}) collective-permute-start(bf16[256,256]{1,0:T(8,128)(2,1)S(1)} %get-tuple-element.25), channel_id=1, source_target_pairs={{0,5},{1,4},{2,7},{3,6},{4,1},{5,0},{6,3},{7,2},{8,13},{9,12},{10,... | collective-permute-start | bytes 393224 | tf_op jit(solution)/shard_map/cond/branch_0_fun/ppermute | solution.py:387
  13.6 6.8 %collective-permute-start.1 = (bf16[256,256]{1,0:T(8,128)(2,1)S(1)}, bf16[256,256]{1,0:T(8,128)(2,1)S(1)}, u32[]{:S(2)}, u32[]{:S(2)}) collective-permute-start(bf16[256,256]{1,0:T(8,128)(2,1)S(1)} %get-tuple-element.25), channel_id=1, source_target_pairs={{0,1},{1,0},{2,3},{3,2},{4,5},{5,4},{6,7},{7,6},{8,9},{9,8},{10,11... | collective-permute-start | bytes 393224 | tf_op jit(solution)/shard_map/cond/branch_0_fun/ppermute | solution.py:386
  14.2 6.0 %collective-permute-start = (bf16[2,2,32,256]{3,2,1,0:T(8,128)(2,1)S(1)}, bf16[2,2,32,256]{3,2,1,0:T(8,128)(2,1)S(1)}, u32[]{:S(2)}, u32[]{:S(2)}) collective-permute-start(bf16[2,2,32,256]{3,2,1,0:T(8,128)(2,1)S(1)} %get-tuple-element.24), channel_id=1, source_target_pairs={{0,4},{2,6},{4,0},{6,2},{8,12},{10,14},{12,8},{14,10},{16,20},{18,... | collective-permute-start | bytes 196616 | tf_op jit(solution)/shard_map/cond/branch_0_fun/ppermute | solution.py:389
  15.8 4.4 %collective-permute-start.3 = (f32[8,128]{1,0:T(8,128)S(1)}, f32[8,128]{1,0:T(8,128)S(1)}, u32[]{:S(2)}, u32[]{:S(2)}) collective-permute-start(f32[8,128]{1,0:T(8,128)S(1)} %get-tuple-element.27.refs_4_), channel_id=1, source_target_pairs={{0,4},{2,6},{4,0},{6,2},{8,12},{10,14},{12,8},{14,10},{16,20},{18,... | collective-permute-start | bytes 12296 | tf_op jit(solution)/shard_map/cond/branch_0_fun/ppermute | solution.py:401
  20.7 1.4 %collective-permute-start.4 = (f32[4,32,256]{2,1,0:T(8,128)S(1)}, f32[4,32,256]{2,1,0:T(8,128)S(1)}, u32[]{:S(2)}, u32[]{:S(2)}) collective-permute-start(f32[4,32,256]{2,1,0:T(8,128)S(1)} %get-tuple-element.29), channel_id=1, source_target_pairs={{0,2},{2,0},{4,6},{6,4},{8,10},{10,8},{12,14},{14,12},{16,18},{18,... | collective-permute-start | bytes 393224 | tf_op jit(solution)/shard_map/cond/branch_0_fun/ppermute | solution.py:337
  22.1 5.9 %collective-permute-start.5 = (f32[1,32,256]{2,1,0:T(8,128)S(1)}, f32[1,32,256]{2,1,0:T(8,128)S(1)}, u32[]{:S(2)}, u32[]{:S(2)}) collective-permute-start(f32[1,32,256]{2,1,0:T(8,128)S(1)} %get-tuple-element.57), channel_id=1, source_target_pairs={{0,24},{2,26},{4,28},{6,30},{8,16},{10,18},{12,20},{14,22},{16,8},... | collective-permute-start | bytes 98312 | tf_op jit(solution)/shard_map/cond/branch_0_fun/ppermute | solution.py:354
  24.3 4.9 %collective-permute-start.7 = (f32[1,32,256]{2,1,0:T(8,128)S(1)}, f32[1,32,256]{2,1,0:T(8,128)S(1)}, u32[]{:S(2)}, u32[]{:S(2)}) collective-permute-start(f32[1,32,256]{2,1,0:T(8,128)S(1)} %get-tuple-element.58), channel_id=1, source_target_pairs={{0,16},{2,18},{4,20},{6,22},{8,24},{10,26},{12,28},{14,30},{16,0},... | collective-permute-start | bytes 98312 | tf_op jit(solution)/shard_map/cond/branch_0_fun/ppermute | solution.py:354
  25.0 4.3 %collective-permute-start.6 = (f32[1,32,256]{2,1,0:T(8,128)S(1)}, f32[1,32,256]{2,1,0:T(8,128)S(1)}, u32[]{:S(2)}, u32[]{:S(2)}) collective-permute-start(f32[1,32,256]{2,1,0:T(8,128)S(1)} %get-tuple-element.59), channel_id=1, source_target_pairs={{0,8},{2,10},{4,12},{6,14},{8,0},{10,2},{12,4},{14,6},{16,24},{18,... | collective-permute-start | bytes 98312 | tf_op jit(solution)/shard_map/cond/branch_0_fun/ppermute | solution.py:354
where the time goes:
time: 30.1 us; the launch traced here: 29.9 us
  starting transfers between devices  15.4 us (51%)
  waiting for transfers between devices  9.25 us (31%)
  local copies, waits for them, and re-layouts  2.37 us (8%)
  Pallas kernels  2.01 us (7%)
  other arithmetic  0.65 us (2%)
    ppermute x1, starting transfers between devices, body(): across = lax.ppermute(design, 'tm', across_pairs)  5.05 us
    ppermute x3, starting transfers between devices, sum_over_groups(): lax.ppermute(share(place ^ d), 'tm', [(i, i ^ d * stride) for i in range(...  4.45 us
    ppermute x1, waiting for transfers between devices, run(): lax.ppermute(rows_here, 'tm', beside_pairs)  4.02 us
    ppermute x3, waiting for transfers between devices, sum_over_groups(): lax.ppermute(share(place ^ d), 'tm', [(i, i ^ d * stride) for i in range(...  2.71 us
    unnamed x12, local copies, waits for them, and re-layouts  2.36 us
    ppermute x1, starting transfers between devices, body(): rows_across = lax.ppermute(rows, 'tm', rows_pairs)  1.79 us
    ppermute x1, starting transfers between devices, run(): lax.ppermute(there, 'tm', beside_pairs)  1.6 us
    ppermute x1, starting transfers between devices, run(): lax.ppermute(every, ('tm', 'col'), both)  1.41 us
  transfers between devices with their start and end apart: 12, of which 7 were waited for; matrix products, arithmetic and copies ran while one was open for 0% of the time, Pallas kernels for 5%

commit v1 on v0

--- a/solution.py
+++ b/solution.py
@@ -330,14 +330,14 @@
     split = columns == 2 and rows_out % 16 == 0 and block_width % (4 * rows_out) == 0
     finish = finish_two if split else finish_any
     total = finish(rows_here, (partial, toeplitz, swapped), ids.reshape(columns), rows_out, swap, beside_pairs)
-    return total * (1.0 / (2.0 * row_count * devices))
+    return total
 
 
 def core_sum(mine, other, swap):
     return mine + lax.ppermute(other, "tm", swap)
 
 
-def sum_over_groups(total, stride, turns=(3, 1, 2)):
+def sum_over_groups(total, stride, count, turns=(3, 1, 2)):
     devices = lax.axis_size("tm")
     index = lax.axis_index("tm")
     left = total.shape[0]
@@ -353,12 +353,13 @@
         for d in turns if group == 4 else (1,):
             total = total + lax.ppermute(share(place ^ d), "tm", [(i, i ^ (d * stride)) for i in range(devices)])
         stride, left = stride * group, left // group
-    return total[0]
+    return total[0] * (1.0 / count)
 
 
 def finish_two(rows_here, blocks, block_ids, rows_out, swap, beside_pairs):
     devices = lax.axis_size("tm")
     length, width = blocks[0].shape
+    count = float(length * devices)
     groups = width // rows_out // 4
     half = jax.ShapeDtypeStruct((groups, 2, rows_out, length), jnp.bfloat16)
     every, here, there = pl.pallas_call(
@@ -407,7 +408,7 @@
                 compiler_params=LIMIT,
                 name="gram",
             )(scaled, *(held[i] for i in order))
-            return sum_over_groups(core_sum(mine, other, swap), 4, (2, 1, 3) if own_block else (3, 1, 2))
+            return sum_over_groups(core_sum(mine, other, swap), 4, count, (2, 1, 3) if own_block else (3, 1, 2))
 
         return run
 
@@ -444,7 +445,7 @@
             compiler_params=LIMIT,
             name="late_mine",
         )(beside_every, both_half, column_half, scaled, mine_early, scaled_beside)
-        return sum_over_groups(core_sum(mine, other, swap), 4, (2, 1, 3))
+        return sum_over_groups(core_sum(mine, other, swap), 4, count, (2, 1, 3))
 
     return lax.cond(block_ids[0] == 0, sums_own, sums(False), every, here, there, rows_here)
 
@@ -452,6 +453,7 @@
 def finish_any(rows_here, blocks, block_ids, rows_out, swap, beside_pairs):
     devices, columns = lax.axis_size("tm"), lax.axis_size("col")
     length, width = blocks[0].shape
+    count = float(length * devices)
     filtered = pl.pallas_call(
         filter_kernel,
         out_shape=jax.ShapeDtypeStruct((width // rows_out // 4, 2, 2, rows_out, length), jnp.bfloat16),
@@ -487,7 +489,7 @@
         compiler_params=LIMIT,
         name="gram",
     )(block_ids, scaled, *held)
-    return sum_over_groups(core_sum(mine, other, swap), 4)
+    return sum_over_groups(core_sum(mine, other, swap), 4, count)
 
 
 def solution(mesh):

time: 30.1 us -> 30.1 us (level)
  other arithmetic: 0.65 us -> 0.03 us
  local copies, waits for them, and re-layouts: 2.37 us -> 2.98 us
    unnamed x12 -> x14, local copies, waits for them, and re-layouts: 2.36 us -> 2.97 us
    mul x1, other arithmetic: 0.62 us -> 0.01 us  [sum_over_groups(): return total[0] * (1.0 / count)]
where the time goes in v1:
time: 30.1 us; the launch traced here: 29.9 us
  starting transfers between devices  15.4 us (51%)
  waiting for transfers between devices  9.25 us (31%)
  local copies, waits for them, and re-layouts  2.98 us (10%)
  Pallas kernels  2.01 us (7%)
    ppermute x1, starting transfers between devices, body(): across = lax.ppermute(design, 'tm', across_pairs)  5.05 us
    ppermute x3, starting transfers between devices, sum_over_groups(): lax.ppermute(share(place ^ d), 'tm', [(i, i ^ d * stride) for i in range(...  4.45 us
    ppermute x1, waiting for transfers between devices, run(): lax.ppermute(rows_here, 'tm', beside_pairs)  4.02 us
    unnamed x14, local copies, waits for them, and re-layouts  2.97 us
    ppermute x3, waiting for transfers between devices, sum_over_groups(): lax.ppermute(share(place ^ d), 'tm', [(i, i ^ d * stride) for i in range(...  2.71 us
    ppermute x1, starting transfers between devices, body(): rows_across = lax.ppermute(rows, 'tm', rows_pairs)  1.79 us
    ppermute x1, starting transfers between devices, run(): lax.ppermute(there, 'tm', beside_pairs)  1.6 us
    ppermute x1, starting transfers between devices, run(): lax.ppermute(every, ('tm', 'col'), both)  1.41 us
  transfers between devices with their start and end apart: 12, of which 7 were waited for; matrix products, arithmetic and copies ran while one was open for 0% of the time, Pallas kernels for 5%

profile of v1, /device:TPU:0, one launch (start us, length us, event | category | flops | bytes accessed | tf_op | source)
XLA Modules:
  0.0 29.9 jit_solution(7179361749507841607)
XLA Ops:
  0.0 5.0 %collective-permute-start.18 = (bf16[128,2,256]{2,1,0:T(2,128)(2,1)}, bf16[128,2,256]{2,1,0:T(2,128)(2,1)S(1)}, u32[]{:S(2)}, u32[]{:S(2)}) collective-permute-start(bf16[128,2,256]{2,1,0:T(2,128)(2,1)} %design_ref.1), channel_id=1, source_target_pairs={{0,24},{2,26},{4,12},{6,14},{8,0},{10,2},{12,20},{14,22},{16,8},{1... | collective-permute-start | bytes 393224 | tf_op jit(solution)/shard_map/ppermute | solution.py:275
  5.1 0.6 %copy-done.4 = s32[128]{0:T(128)S(1)} copy-done((s32[128]{0:T(128)S(1)}, s32[128]{0:T(128)}, u32[]{:S(2)}) %copy-start.4) | copy-done | bytes 536
  5.7 0.0 copy-done.5
  5.7 0.0 copy-done.2
  5.8 1.8 %collective-permute-start.16 = (f32[8,128]{1,0:T(8,128)S(1)}, f32[8,128]{1,0:T(8,128)S(1)}, u32[]{:S(2)}, u32[]{:S(2)}) collective-permute-start(f32[8,128]{1,0:T(8,128)S(1)} %get-tuple-element.49.rows_ref), channel_id=1, source_target_pairs={{0,24},{2,26},{4,12},{6,14},{8,0},{10,2},{12,4},{14,6},{16,8},{18,... | collective-permute-start | bytes 12296 | tf_op jit(solution)/shard_map/ppermute | solution.py:288
  7.6 0.9 %copy-done = bf16[128,2,256]{2,1,0:T(2,128)(2,1)S(1)} copy-done((bf16[128,2,256]{2,1,0:T(2,128)(2,1)S(1)}, bf16[128,2,256]{2,1,0:T(2,128)(2,1)}, u32[]{:S(2)}) %copy-start) | copy-done | bytes 131096
  8.5 0.8 %copy-done.1 = bf16[16,2,512]{2,1,0:T(2,128)(2,1)S(1)} copy-done((bf16[16,2,512]{2,1,0:T(2,128)(2,1)S(1)}, bf16[16,2,512]{2,1,0:T(2,128)(2,1)}, u32[]{:S(2)}) %copy-start.1) | copy-done | bytes 32792
  9.3 0.3 prepare.1
  9.6 0.7 %collective-permute-done.17.beside_ref = bf16[128,2,256]{2,1,0:T(2,128)(2,1)S(1)} collective-permute-done((bf16[128,2,256]{2,1,0:T(2,128)(2,1)}, bf16[128,2,256]{2,1,0:T(2,128)(2,1)S(1)}, u32[]{:S(2)}, u32[]{:S(2)}) %collective-permute-start.17) | collective-permute-done | bytes 131104 | tf_op jit(solution)/shard_map/ppermute | solution.py:289
  10.3 0.1 collective-permute-start.19
  10.3 0.5 %toeplitz.1 = (bf16[5,256,256]{2,1,0:T(8,128)(2,1)S(1)}, f32[8,128]{1,0:T(8,128)S(1)}) custom-call(f32[8,128]{1,0:T(8,128)S(1)} %get-tuple-element.49.rows_ref, f32[8,128]{1,0:T(8,128)S(1)} %collective-permute-done.16.rows_across_ref, bf16[32,1280]{1,0:T(8,128)(2,1)S(1)} %get-tuple-element.50.spread_ref), custom_call_target="tpu_custom_call" | custom-call | flops 20000000000 | bytes 1048576 | tf_op jit(solution)/shard_map/toeplitz/pallas_call | solution.py:301
  10.8 0.3 %partial.1.partial_ref = f32[256,256]{1,0:T(8,128)S(1)} custom-call(bf16[5,256,256]{2,1,0:T(8,128)(2,1)S(1)} %get-tuple-element.51.toeplitz_ref, bf16[128,2,256]{2,1,0:T(2,128)(2,1)S(1)} %collective-permute-done.17.beside_ref, bf16[128,2,256]{2,1,0:T(2,128)(2,1)S(1)} %get-tuple-element.52.own_ref, bf16[128,2,256]{2,1,0:T(2,128)(2,1)S(1)} %collective-permute-done.18.across_ref), custom_call_target="tpu_custom_call" | custom-call | tf_op jit(solution)/shard_map/partial/pallas_call | solution.py:322
  11.2 0.7 %collective-permute-done.19.swapped_ref = bf16[2,128,2,256]{3,2,1,0:T(2,128)(2,1)S(1)} collective-permute-done((bf16[2,128,2,256]{3,2,1,0:T(2,128)(2,1)S(1)}, bf16[2,128,2,256]{3,2,1,0:T(2,128)(2,1)S(1)}, u32[]{:S(2)}, u32[]{:S(2)}) %collective-permute-start.19) | collective-permute-done | bytes 262176 | tf_op jit(solution)/shard_map/ppermute | solution.py:321
  11.9 0.3 %filter.1 = (bf16[256,256]{1,0:T(8,128)(2,1)S(1)}, bf16[2,2,32,256]{3,2,1,0:T(8,128)(2,1)S(1)}, bf16[2,2,32,256]{3,2,1,0:T(8,128)(2,1)S(1)}) custom-call(f32[256,256]{1,0:T(8,128)S(1)} %partial.1.partial_ref, bf16[5,256,256]{2,1,0:T(8,128)(2,1)S(1)} %get-tuple-element.51.toeplitz_ref, bf16[2,128,2,256]{3,2,1,0:T(2,128)(2,1)S(1)} %collective-permute-done.19.swapped_ref), custom_call_target="tpu_custom_call" | custom-call | tf_op jit(solution)/shard_map/filter/pallas_call | solution.py:365
  12.2 17.1 %conditional.1 = (f32[32,256]{1,0:T(8,128)S(1)}) conditional(s32[]{:T(128)} %bitcast.5, (bf16[2,2,32,256]{3,2,1,0:T(8,128)(2,1)S(1)}, bf16[256,256]{1,0:T(8,128)(2,1)S(1)}, f32[8,128]{1,0:T(8,128)S(1)}, bf16[2,2,32,256]{3,2,1,0:T(8,128)(2,1)S(1)}) %tuple.11, (bf16[256,256]{1,0:T(8,128)(2,1)S(1)}, bf16[2,2,32,256]{3,2,1,0:T(8,128)(2,1)S(1)}, ...), branch_computations={%region_0.1_spmd, %region_1.2_spmd} | conditional | flops 65580 | bytes 2999079 | solution.py:450
  12.2 1.4 %collective-permute-start.2 = (bf16[256,256]{1,0:T(8,128)(2,1)S(1)}, bf16[256,256]{1,0:T(8,128)(2,1)S(1)}, u32[]{:S(2)}, u32[]{:S(2)}) collective-permute-start(bf16[256,256]{1,0:T(8,128)(2,1)S(1)} %get-tuple-element.25), channel_id=1, source_target_pairs={{0,5},{1,4},{2,7},{3,6},{4,1},{5,0},{6,3},{7,2},{8,13},{9,12},{10,... | collective-permute-start | bytes 393224 | tf_op jit(solution)/shard_map/cond/branch_0_fun/ppermute | solution.py:388
  13.6 0.5 %collective-permute-start.1 = (bf16[256,256]{1,0:T(8,128)(2,1)S(1)}, bf16[256,256]{1,0:T(8,128)(2,1)S(1)}, u32[]{:S(2)}, u32[]{:S(2)}) collective-permute-start(bf16[256,256]{1,0:T(8,128)(2,1)S(1)} %get-tuple-element.25), channel_id=1, source_target_pairs={{0,1},{1,0},{2,3},{3,2},{4,5},{5,4},{6,7},{7,6},{8,9},{9,8},{10,11... | collective-permute-start | bytes 393224 | tf_op jit(solution)/shard_map/cond/branch_0_fun/ppermute | solution.py:387
  14.2 1.6 %collective-permute-start = (bf16[2,2,32,256]{3,2,1,0:T(8,128)(2,1)S(1)}, bf16[2,2,32,256]{3,2,1,0:T(8,128)(2,1)S(1)}, u32[]{:S(2)}, u32[]{:S(2)}) collective-permute-start(bf16[2,2,32,256]{3,2,1,0:T(8,128)(2,1)S(1)} %get-tuple-element.24), channel_id=1, source_target_pairs={{0,4},{2,6},{4,0},{6,2},{8,12},{10,14},{12,8},{14,10},{16,20},{18,... | collective-permute-start | bytes 196616 | tf_op jit(solution)/shard_map/cond/branch_0_fun/ppermute | solution.py:390
  15.8 0.4 %collective-permute-start.3 = (f32[8,128]{1,0:T(8,128)S(1)}, f32[8,128]{1,0:T(8,128)S(1)}, u32[]{:S(2)}, u32[]{:S(2)}) collective-permute-start(f32[8,128]{1,0:T(8,128)S(1)} %get-tuple-element.27.refs_4_), channel_id=1, source_target_pairs={{0,4},{2,6},{4,0},{6,2},{8,12},{10,14},{12,8},{14,10},{16,20},{18,... | collective-permute-start | bytes 12296 | tf_op jit(solution)/shard_map/cond/branch_0_fun/ppermute | solution.py:402
  16.2 4.0 %collective-permute-done.3.refs_5_ = f32[8,128]{1,0:T(8,128)S(1)} collective-permute-done((f32[8,128]{1,0:T(8,128)S(1)}, f32[8,128]{1,0:T(8,128)S(1)}, u32[]{:S(2)}, u32[]{:S(2)}) %collective-permute-start.3) | collective-permute-done | bytes 4128 | tf_op jit(solution)/shard_map/cond/branch_0_fun/ppermute | solution.py:402
  20.2 0.2 collective-permute-done.1.refs_1_
  20.4 0.3 scale.1
  20.7 0.1 collective-permute-start.4
  20.8 0.3 gram.1
  21.1 1.0 %collective-permute-done.4 = f32[4,32,256]{2,1,0:T(8,128)S(1)} collective-permute-done((f32[4,32,256]{2,1,0:T(8,128)S(1)}, f32[4,32,256]{2,1,0:T(8,128)S(1)}, u32[]{:S(2)}, u32[]{:S(2)}) %collective-permute-start.4) | collective-permute-done | bytes 131104 | tf_op jit(solution)/shard_map/cond/branch_0_fun/ppermute | solution.py:337
  22.1 2.2 %collective-permute-start.5 = (f32[1,32,256]{2,1,0:T(8,128)S(1)}, f32[1,32,256]{2,1,0:T(8,128)S(1)}, u32[]{:S(2)}, u32[]{:S(2)}) collective-permute-start(f32[1,32,256]{2,1,0:T(8,128)S(1)} %get-tuple-element.58), channel_id=1, source_target_pairs={{0,24},{2,26},{4,28},{6,30},{8,16},{10,18},{12,20},{14,22},{16,8},... | collective-permute-start | bytes 98312 | tf_op jit(solution)/shard_map/cond/branch_0_fun/ppermute | solution.py:354
  24.3 0.7 %collective-permute-start.7 = (f32[1,32,256]{2,1,0:T(8,128)S(1)}, f32[1,32,256]{2,1,0:T(8,128)S(1)}, u32[]{:S(2)}, u32[]{:S(2)}) collective-permute-start(f32[1,32,256]{2,1,0:T(8,128)S(1)} %get-tuple-element.59), channel_id=1, source_target_pairs={{0,16},{2,18},{4,20},{6,22},{8,24},{10,26},{12,28},{14,30},{16,0},... | collective-permute-start | bytes 98312 | tf_op jit(solution)/shard_map/cond/branch_0_fun/ppermute | solution.py:354
  25.0 1.6 %collective-permute-start.6 = (f32[1,32,256]{2,1,0:T(8,128)S(1)}, f32[1,32,256]{2,1,0:T(8,128)S(1)}, u32[]{:S(2)}, u32[]{:S(2)}) collective-permute-start(f32[1,32,256]{2,1,0:T(8,128)S(1)} %get-tuple-element.60), channel_id=1, source_target_pairs={{0,8},{2,10},{4,12},{6,14},{8,0},{10,2},{12,4},{14,6},{16,24},{18,... | collective-permute-start | bytes 98312 | tf_op jit(solution)/shard_map/cond/branch_0_fun/ppermute | solution.py:354
  26.6 1.5 %collective-permute-done.5 = f32[1,32,256]{2,1,0:T(8,128)S(1)} collective-permute-done((f32[1,32,256]{2,1,0:T(8,128)S(1)}, f32[1,32,256]{2,1,0:T(8,128)S(1)}, u32[]{:S(2)}, u32[]{:S(2)}) %collective-permute-start.5) | collective-permute-done | bytes 32800 | tf_op jit(solution)/shard_map/cond/branch_0_fun/ppermute | solution.py:354
  28.0 1.2 %collective-permute-done.7 = f32[1,32,256]{2,1,0:T(8,128)S(1)} collective-permute-done((f32[1,32,256]{2,1,0:T(8,128)S(1)}, f32[1,32,256]{2,1,0:T(8,128)S(1)}, u32[]{:S(2)}, u32[]{:S(2)}) %collective-permute-start.7) | collective-permute-done | bytes 32800 | tf_op jit(solution)/shard_map/cond/branch_0_fun/ppermute | solution.py:354
  29.3 0.0 collective-permute-done.6
  29.3 0.6 %copy-done.6 = f32[32,256]{1,0:T(8,128)} copy-done((f32[32,256]{1,0:T(8,128)}, f32[32,256]{1,0:T(8,128)S(1)}, u32[]{:S(2)}) %copy-start.6) | copy-done | bytes 32792
  (18 shorter events, 0.1 us)
Async XLA Ops:
  0.0 9.6 %collective-permute-start.18 = (bf16[128,2,256]{2,1,0:T(2,128)(2,1)}, bf16[128,2,256]{2,1,0:T(2,128)(2,1)S(1)}, u32[]{:S(2)}, u32[]{:S(2)}) collective-permute-start(bf16[128,2,256]{2,1,0:T(2,128)(2,1)} %design_ref.1), channel_id=1, source_target_pairs={{0,24},{2,26},{4,12},{6,14},{8,0},{10,2},{12,20},{14,22},{16,8},{1... | collective-permute-start | bytes 393224 | tf_op jit(solution)/shard_map/ppermute | solution.py:275
  5.0 5.2 %collective-permute-start.17 = (bf16[128,2,256]{2,1,0:T(2,128)(2,1)}, bf16[128,2,256]{2,1,0:T(2,128)(2,1)S(1)}, u32[]{:S(2)}, u32[]{:S(2)}) collective-permute-start(bf16[128,2,256]{2,1,0:T(2,128)(2,1)} %design_ref.1), channel_id=1, source_target_pairs={{0,4},{2,6},{4,0},{6,2},{8,12},{10,14},{12,8},{14,10},{16,20},{18,... | collective-permute-start | bytes 393224 | tf_op jit(solution)/shard_map/ppermute | solution.py:289
  5.1 0.7 %copy-start.4 = (s32[128]{0:T(128)S(1)}, s32[128]{0:T(128)}, u32[]{:S(2)}) copy-start(s32[128]{0:T(128)} %param.10) | copy-start | bytes 1540
  5.1 0.7 %copy-start.5 = (s32[2]{0:T(128)S(1)}, s32[2]{0:T(128)}, u32[]{:S(2)}) copy-start(s32[2]{0:T(128)} %param.13) | copy-start | bytes 28
  5.1 0.7 %copy-start.2 = (f32[2,128]{1,0:T(2,128)S(1)}, f32[2,128]{1,0:T(2,128)}, u32[]{:S(2)}) copy-start(f32[2,128]{1,0:T(2,128)} %weights_ref.1) | copy-start | bytes 3076
  5.1 0.7 %copy-start.3 = (s32[128]{0:T(128)S(1)}, s32[128]{0:T(128)}, u32[]{:S(2)}) copy-start(s32[128]{0:T(128)} %param.11) | copy-start | bytes 1540
  5.8 4.6 %collective-permute-start.16 = (f32[8,128]{1,0:T(8,128)S(1)}, f32[8,128]{1,0:T(8,128)S(1)}, u32[]{:S(2)}, u32[]{:S(2)}) collective-permute-start(f32[8,128]{1,0:T(8,128)S(1)} %get-tuple-element.49.rows_ref), channel_id=1, source_target_pairs={{0,24},{2,26},{4,12},{6,14},{8,0},{10,2},{12,4},{14,6},{16,8},{18,... | collective-permute-start | bytes 12296 | tf_op jit(solution)/shard_map/ppermute | solution.py:288
  7.6 0.9 %copy-start = (bf16[128,2,256]{2,1,0:T(2,128)(2,1)S(1)}, bf16[128,2,256]{2,1,0:T(2,128)(2,1)}, u32[]{:S(2)}) copy-start(bf16[128,2,256]{2,1,0:T(2,128)(2,1)} %design_ref.1) | copy-start | bytes 393220
  8.5 0.8 %copy-start.1 = (bf16[16,2,512]{2,1,0:T(2,128)(2,1)S(1)}, bf16[16,2,512]{2,1,0:T(2,128)(2,1)}, u32[]{:S(2)}) copy-start(bf16[16,2,512]{2,1,0:T(2,128)(2,1)} %taps_ref.1) | copy-start | bytes 98308
  10.3 1.6 %collective-permute-start.19 = (bf16[2,128,2,256]{3,2,1,0:T(2,128)(2,1)S(1)}, bf16[2,128,2,256]{3,2,1,0:T(2,128)(2,1)S(1)}, u32[]{:S(2)}, u32[]{:S(2)}) collective-permute-start(bf16[2,128,2,256]{3,2,1,0:T(2,128)(2,1)S(1)} %choose.1), channel_id=1, source_target_pairs={{0,2},{2,0},{4,6},{6,4},{8,10},{10,8},{12,14},{14,12},{16,18},{18,... | collective-permute-start | bytes 786440 | tf_op jit(solution)/shard_map/ppermute | solution.py:321
  12.2 8.0 %collective-permute-start.2 = (bf16[256,256]{1,0:T(8,128)(2,1)S(1)}, bf16[256,256]{1,0:T(8,128)(2,1)S(1)}, u32[]{:S(2)}, u32[]{:S(2)}) collective-permute-start(bf16[256,256]{1,0:T(8,128)(2,1)S(1)} %get-tuple-element.25), channel_id=1, source_target_pairs={{0,5},{1,4},{2,7},{3,6},{4,1},{5,0},{6,3},{7,2},{8,13},{9,12},{10,... | collective-permute-start | bytes 393224 | tf_op jit(solution)/shard_map/cond/branch_0_fun/ppermute | solution.py:388
  13.6 6.8 %collective-permute-start.1 = (bf16[256,256]{1,0:T(8,128)(2,1)S(1)}, bf16[256,256]{1,0:T(8,128)(2,1)S(1)}, u32[]{:S(2)}, u32[]{:S(2)}) collective-permute-start(bf16[256,256]{1,0:T(8,128)(2,1)S(1)} %get-tuple-element.25), channel_id=1, source_target_pairs={{0,1},{1,0},{2,3},{3,2},{4,5},{5,4},{6,7},{7,6},{8,9},{9,8},{10,11... | collective-permute-start | bytes 393224 | tf_op jit(solution)/shard_map/cond/branch_0_fun/ppermute | solution.py:387
  14.2 6.0 %collective-permute-start = (bf16[2,2,32,256]{3,2,1,0:T(8,128)(2,1)S(1)}, bf16[2,2,32,256]{3,2,1,0:T(8,128)(2,1)S(1)}, u32[]{:S(2)}, u32[]{:S(2)}) collective-permute-start(bf16[2,2,32,256]{3,2,1,0:T(8,128)(2,1)S(1)} %get-tuple-element.24), channel_id=1, source_target_pairs={{0,4},{2,6},{4,0},{6,2},{8,12},{10,14},{12,8},{14,10},{16,20},{18,... | collective-permute-start | bytes 196616 | tf_op jit(solution)/shard_map/cond/branch_0_fun/ppermute | solution.py:390
  15.8 4.4 %collective-permute-start.3 = (f32[8,128]{1,0:T(8,128)S(1)}, f32[8,128]{1,0:T(8,128)S(1)}, u32[]{:S(2)}, u32[]{:S(2)}) collective-permute-start(f32[8,128]{1,0:T(8,128)S(1)} %get-tuple-element.27.refs_4_), channel_id=1, source_target_pairs={{0,4},{2,6},{4,0},{6,2},{8,12},{10,14},{12,8},{14,10},{16,20},{18,... | collective-permute-start | bytes 12296 | tf_op jit(solution)/shard_map/cond/branch_0_fun/ppermute | solution.py:402
  20.7 1.4 %collective-permute-start.4 = (f32[4,32,256]{2,1,0:T(8,128)S(1)}, f32[4,32,256]{2,1,0:T(8,128)S(1)}, u32[]{:S(2)}, u32[]{:S(2)}) collective-permute-start(f32[4,32,256]{2,1,0:T(8,128)S(1)} %get-tuple-element.29), channel_id=1, source_target_pairs={{0,2},{2,0},{4,6},{6,4},{8,10},{10,8},{12,14},{14,12},{16,18},{18,... | collective-permute-start | bytes 393224 | tf_op jit(solution)/shard_map/cond/branch_0_fun/ppermute | solution.py:337
  22.1 5.9 %collective-permute-start.5 = (f32[1,32,256]{2,1,0:T(8,128)S(1)}, f32[1,32,256]{2,1,0:T(8,128)S(1)}, u32[]{:S(2)}, u32[]{:S(2)}) collective-permute-start(f32[1,32,256]{2,1,0:T(8,128)S(1)} %get-tuple-element.58), channel_id=1, source_target_pairs={{0,24},{2,26},{4,28},{6,30},{8,16},{10,18},{12,20},{14,22},{16,8},... | collective-permute-start | bytes 98312 | tf_op jit(solution)/shard_map/cond/branch_0_fun/ppermute | solution.py:354
  24.3 4.9 %collective-permute-start.7 = (f32[1,32,256]{2,1,0:T(8,128)S(1)}, f32[1,32,256]{2,1,0:T(8,128)S(1)}, u32[]{:S(2)}, u32[]{:S(2)}) collective-permute-start(f32[1,32,256]{2,1,0:T(8,128)S(1)} %get-tuple-element.59), channel_id=1, source_target_pairs={{0,16},{2,18},{4,20},{6,22},{8,24},{10,26},{12,28},{14,30},{16,0},... | collective-permute-start | bytes 98312 | tf_op jit(solution)/shard_map/cond/branch_0_fun/ppermute | solution.py:354
  25.0 4.3 %collective-permute-start.6 = (f32[1,32,256]{2,1,0:T(8,128)S(1)}, f32[1,32,256]{2,1,0:T(8,128)S(1)}, u32[]{:S(2)}, u32[]{:S(2)}) collective-permute-start(f32[1,32,256]{2,1,0:T(8,128)S(1)} %get-tuple-element.60), channel_id=1, source_target_pairs={{0,8},{2,10},{4,12},{6,14},{8,0},{10,2},{12,4},{14,6},{16,24},{18,... | collective-permute-start | bytes 98312 | tf_op jit(solution)/shard_map/cond/branch_0_fun/ppermute | solution.py:354
  29.3 0.6 %copy-start.6 = (f32[32,256]{1,0:T(8,128)}, f32[32,256]{1,0:T(8,128)S(1)}, u32[]{:S(2)}) copy-start(f32[32,256]{1,0:T(8,128)S(1)} %get-tuple-element.96) | copy-start | bytes 98308
